TPU v7x, 256 devices: a whole 4x4x8 slice. The times are simulated.
256 devices in a mesh: clip: 16 (over z_hi, y), seq: 16 (over x, z_lo, core).
Axes of the slice: x: 4, y: 4, z: 8 (z_hi: 4, z_lo: 2; z = z_hi * 2 + z_lo), core: 2. Of those that a mesh axis runs over, the one named last changes fastest.
Arguments:
- space_query: bfloat16 [16, 16, 256, 1152], P('clip', 'seq'), may hold values from -2.5 to 2.5
- space_keys: bfloat16 [16, 16, 256, 1152], P('clip', 'seq'), may hold values from -2.5 to 2.5
- space_values: bfloat16 [16, 16, 256, 1152], P('clip', 'seq'), may hold values from -6 to 6
- space_output: bfloat16 [16, 16, 256, 1152], P('clip', 'seq'), may hold values from -6 to 6
- space_logsum: float32 [16, 16, 16, 256], P('clip', 'seq'), may hold values from 4.5 to 6.5
- time_query: bfloat16 [16, 16, 256, 1152], P('clip', 'seq'), may hold values from -2.5 to 2.5
- time_keys: bfloat16 [16, 16, 256, 1152], P('clip', 'seq'), may hold values from -2.5 to 2.5
- time_values: bfloat16 [16, 16, 256, 1152], P('clip', 'seq'), may hold values from -6 to 6
- time_output: bfloat16 [16, 16, 256, 1152], P('clip', 'seq'), may hold values from -6 to 6
- time_logsum: float32 [16, 256, 16, 16], P('clip', 'seq'), may hold values from 2 to 4
- upstream: bfloat16 [16, 16, 256, 1152], P('clip', 'seq'), may hold values from -6 to 6
- space_weight: bfloat16 [1152, 1152], P('seq'), may hold values from -0.1875 to 0.1875
- time_weight: bfloat16 [1152, 1152], P('seq'), may hold values from -0.1875 to 0.1875
Outputs:
- dquery_space: bfloat16 [16, 16, 256, 1152], P('clip', 'seq')
- dkeys_space: bfloat16 [16, 16, 256, 1152], P('clip', 'seq')
- dvalue_space: bfloat16 [16, 16, 256, 1152], P('clip', 'seq')
- dquery_time: bfloat16 [16, 16, 256, 1152], P('clip', 'seq')
- dkeys_time: bfloat16 [16, 16, 256, 1152], P('clip', 'seq')
- dvalue_time: bfloat16 [16, 16, 256, 1152], P('clip', 'seq')
- dweight_space: float32 [1152, 1152], P('seq', 'clip')
- dweight_time: float32 [1152, 1152], P('seq', 'clip')
All inputs are finite; a program needn't handle non-finite values.
Results may differ from a plain program's by a relative error of at most 0.006.
Values may be sent and summed in bfloat16 or wider, within the bound.
A program may use at most 192 MiB of HBM per device.

v0:
```python
import math

import jax
import jax.numpy as jnp
from jax import lax
from jax.experimental import pallas as pl
from jax.experimental.pallas import tpu as pltpu
from jax.sharding import PartitionSpec as P

BF16 = jnp.bfloat16
F32 = jnp.float32
HEADS = 16
HEAD = 72
D = HEADS * HEAD
S = 256
SEQ = 16
POS = S // SEQ
CHIPS = 8
YS = 4
ZHS = 4
CHIP_ROWS = 2 * HEAD
YROWS = ZHS * HEAD
WIDE = 384
GROUPS = ((0, 6), (6, 11), (11, 16))
FORWARD = ((0, 512), (512, 896), (896, 1152))
BACK = ((0, 384), (384, 768), (768, 1152))
NT = (((1,), (1,)), ((), ()))
TN = (((0,), (0,)), ((), ()))
NN = (((1,), (0,)), ((), ()))


def mm(a, b, dims):
    return lax.dot_general(a, b, dims, preferred_element_type=F32)


def kernel(
    up, tq, tk, tv, so, to, sq, sk, sv, ws, wt, slog, tlog,
    osq, osk, osv, otq, otk, otv, ows, owt,
    X, R, O, SI, GT, GS, TD, TE, SD, W, wown, w32, w32r,
    ind, bias, cen, cenr, cent, cens,
    ut, utp, mine, psend, prec, ysend, yrecv, xzsend, xzrecv, zs, zr,
    ld, own_sem, wp_s, wp_r, w1_s, w1_r, lf_s, lf_r, w2_s, w2_r, w3_s, w3_r, l3_s, l3_r,
    a_s, a_r, c_s, c_r, b_s, b_r, pp_s, pp_r, y_s, y_r, xz_s, xz_r, z_s, z_r, out_sem,
):
    clip = lax.axis_index("clip")
    seq = lax.axis_index("seq")
    y = lax.rem(clip, YS)
    zh = lax.div(clip, YS)
    core = lax.rem(seq, 2)
    chip = lax.div(seq, 2)
    sibling = seq + 1 - 2 * core
    corner = zh * 2 + core

    def seq_peer(k):
        return lax.rem(seq + k, SEQ)

    def chip_peer(k):
        return 2 * lax.rem(chip + k, CHIPS) + core

    def y_peer(k):
        return zh * YS + lax.rem(y + k, YS)

    def z_peer(k):
        other = lax.rem(corner + k, 2 * ZHS)
        return lax.div(other, 2), lax.rem(other, 2)

    def remote(src, dst, send, recv, **where):
        return pltpu.make_async_remote_copy(
            src_ref=src, dst_ref=dst, send_sem=send, recv_sem=recv,
            device_id=where, device_id_type=pl.DeviceIdType.MESH,
        )

    def drain(ref, sem):
        pltpu.make_async_copy(ref, ref, sem).wait()

    barrier = pltpu.get_barrier_semaphore()
    for k in range(1, SEQ):
        pl.semaphore_signal(barrier, inc=1, device_id={"seq": seq_peer(k)}, device_id_type=pl.DeviceIdType.MESH)
    for k in range(1, YS):
        pl.semaphore_signal(barrier, inc=1, device_id={"clip": y_peer(k)}, device_id_type=pl.DeviceIdType.MESH)
    for k in range(1, 2 * ZHS):
        to_zh, to_core = z_peer(k)
        pl.semaphore_signal(
            barrier, inc=1, device_id={"clip": to_zh * YS + y, "seq": 2 * chip + to_core},
            device_id_type=pl.DeviceIdType.MESH,
        )

    loads = [
        pltpu.make_async_copy(src, dst, ld.at[n])
        for n, (src, dst) in enumerate((
            (up, X.at[0]), (tq, X.at[1]), (tk, X.at[2]), (tv, X.at[3]), (so, O.at[0]), (to, O.at[1]),
            (sq, SI.at[0]), (sk, SI.at[1]), (sv, SI.at[2]),
        ))
    ]
    for load in loads:
        load.start()
    w32[0] = wt[...].astype(F32)
    w32[1] = ws[...].astype(F32)

    pl.semaphore_wait(barrier, (SEQ - 1) + (YS - 1) + (2 * ZHS - 1))

    pair = remote(w32, w32r, wp_s, wp_r, seq=sibling)
    pair.start()

    loads[0].wait()
    row_me = pl.ds(pl.multiple_of(seq * POS, POS), POS)

    def rows_of(d):
        return pl.ds(pl.multiple_of(d * POS, POS), POS)

    def send_up(k, carry):
        d = seq_peer(k)
        remote(X.at[0, rows_of(d)], R.at[0, row_me], a_s.at[0], a_r.at[0], seq=d).start()
        return carry

    lax.fori_loop(1, SEQ, send_up, 0)
    own_up = pltpu.make_async_copy(X.at[0, row_me], R.at[0, row_me], own_sem.at[0])
    own_up.start()

    head_row = lax.broadcasted_iota(jnp.int32, (128, D), 0) * HEAD
    column = lax.broadcasted_iota(jnp.int32, (128, D), 1)
    ind[...] = jnp.where((column >= head_row) & (column < head_row + HEAD), 1.0, 0.0).astype(BF16)

    pair.wait()
    chip_rows = pl.ds(pl.multiple_of(chip * CHIP_ROWS, 16), CHIP_ROWS)
    tile = pl.ds(pl.multiple_of((2 * y + core) * 128, 128), 128)
    last = pl.ds(D - 128, 128)
    for m in range(2):
        first, second = w32[m], w32r[m]
        low = jnp.where(core == 0, first, second)
        high = jnp.where(core == 0, second, first)
        wown[m] = jnp.concatenate((low, high), axis=0).astype(BF16)
    def stage1(m):
        W[m, chip_rows, tile] = wown[m, :, tile]

        def one(k, carry):
            remote(wown.at[m, :, tile], W.at[m, chip_rows, tile], w1_s.at[m], w1_r.at[m], seq=chip_peer(k)).start()
            return carry

        lax.fori_loop(1, CHIPS, one, 0)

    stage1(0)
    W[core, chip_rows, last] = wown[core, :, last]

    def send_last(k, carry):
        remote(wown.at[core, :, last], W.at[core, chip_rows, last], lf_s, lf_r, seq=chip_peer(k)).start()
        return carry

    lax.fori_loop(1, CHIPS, send_last, 0)

    for n in (1, 2, 3):
        loads[n].wait()
    for g, (begin, end) in enumerate(FORWARD):
        columns = pl.ds(begin, end - begin)

        def send_group(k, carry, g=g, columns=columns):
            d = seq_peer(k)
            remote(
                X.at[1:4, rows_of(d), columns], R.at[1:4, row_me, columns], a_s.at[1 + g], a_r.at[1 + g], seq=d
            ).start()
            return carry

        lax.fori_loop(1, SEQ, send_group, 0)
    own_rest = pltpu.make_async_copy(X.at[1:4, row_me], R.at[1:4, row_me], own_sem.at[1])
    own_rest.start()
    stage1(1)

    for n in range(D // 128):
        ut[128 * n:128 * (n + 1), :] = X[0, :, 128 * n:128 * (n + 1)].astype(F32).T
    for j in range(YS):
        utp[j] = jnp.concatenate(
            [ut[HEAD * (YS * i + j):HEAD * (YS * i + j + 1), :] for i in range(ZHS)], axis=0
        ).astype(BF16)
    loads[4].wait()
    loads[5].wait()
    factor = 1.0 / math.sqrt(lax.axis_size("clip") * SEQ * S)

    def gradient(k):
        rows = utp[lax.rem(y + k, YS)]

        def piece(n, carry):
            columns = pl.ds(pl.multiple_of(n * WIDE, 128), WIDE)
            psend[k, :, columns] = (mm(rows, O[1 - core, :, columns], NN) * factor).astype(BF16)
            mine[k, :, columns] = mm(rows, O[core, :, columns], NN) * factor
            return carry

        lax.fori_loop(0, D // WIDE, piece, 0)
        remote(psend.at[k], prec.at[k], pp_s.at[k], pp_r.at[k], seq=sibling).start()

    def stage2(m):
        drain(W.at[m, 0:(CHIPS - 1) * CHIP_ROWS, 0:128], w1_r.at[m])
        remote(W.at[m, :, tile], W.at[m, :, tile], w3_s.at[m], w3_r.at[m], seq=sibling).start()
        for k in range(1, YS):
            remote(W.at[m, :, tile], W.at[m, :, tile], w2_s.at[m], w2_r.at[m], clip=y_peer(k)).start()

    def stage3(m):
        drain(W.at[m, :, 0:384], w2_r.at[m])
        for k in range(1, YS):
            there = pl.ds(pl.multiple_of((2 * lax.rem(y + k, YS) + core) * 128, 128), 128)
            remote(W.at[m, :, there], W.at[m, :, there], w3_s.at[m], w3_r.at[m], seq=sibling).start()
        drain(W.at[m, :, 0:512], w3_r.at[m])

    gradient(2)
    stage2(0)
    drain(W.at[0, 0:(CHIPS - 1) * CHIP_ROWS, 0:128], lf_r)
    remote(W.at[core, :, last], W.at[core, :, last], l3_s, l3_r, seq=sibling).start()
    gradient(1)
    gradient(3)
    for k in (2, 1, 3):
        drain(prec.at[k], pp_r.at[k])
        ysend[k - 1] = (mine[k] + prec[k].astype(F32)).astype(BF16)
        remote(ysend.at[k - 1], yrecv.at[k - 1], y_s.at[k - 1], y_r.at[k - 1], clip=y_peer(k)).start()
    gradient(0)
    stage2(1)

    zeros = jnp.zeros((S, D), BF16)
    for n in range(3):
        TD[n] = zeros
        SD[n] = zeros
    position = lax.broadcasted_iota(jnp.int32, (S, S), 0)
    other = lax.broadcasted_iota(jnp.int32, (S, S), 1)
    bias[...] = jnp.where(lax.rem(position, POS) == lax.rem(other, POS), 0.0, -1e30)

    stage3(0)
    drain(W.at[0, :, last], l3_r)

    def project(tokens, m, n):
        return mm(tokens, W[m, n * WIDE:(n + 1) * WIDE, :], NT).astype(BF16)

    def split(grad, outputs):
        product = grad.astype(F32) * outputs.astype(F32)
        high = product.astype(BF16)
        return high, (product - high.astype(F32)).astype(BF16)

    total = jnp.zeros((S, 128), F32)
    for n in range(D // WIDE):
        columns = slice(n * WIDE, (n + 1) * WIDE)
        high, low = split(project(X[0], 0, n), O[1, :, columns])
        total = total + (mm(high, ind[:, columns], NT) + mm(low, ind[:, columns], NT))
    cen[...] = total

    def send_center(k, carry):
        d = seq_peer(k)
        remote(cen.at[rows_of(d)], cenr.at[row_me], c_s, c_r, seq=d).start()
        return carry

    lax.fori_loop(1, SEQ, send_center, 0)
    own_cen = pltpu.make_async_copy(cen.at[row_me], cenr.at[row_me], own_sem.at[2])
    own_cen.start()

    others = (SEQ - 1) * POS
    own_up.wait()
    drain(R.at[0, 0:others], a_r.at[0])
    for n in range(D // WIDE):
        GT[:, n * WIDE:(n + 1) * WIDE] = project(R[0], 0, n)
    own_cen.wait()
    drain(cenr.at[0:others], c_r)
    cent[...] = cenr[...].T

    scale = 1.0 / math.sqrt(HEAD)
    lane = lax.broadcasted_iota(jnp.int32, (16, 256), 1)

    def heads(first, end, q_ref, k_ref, v_ref, g_ref, log_ref, center_ref, masked, out):
        def one(h, carry):
            offset = jnp.minimum(lax.div(h * HEAD, 128), D // 128 - 2) * 128
            window = pl.ds(pl.multiple_of(offset, 128), 256)
            begin = h * HEAD - offset
            keep = jnp.where((lane >= begin) & (lane < begin + HEAD), 1.0, 0.0).astype(BF16)
            keep = jnp.broadcast_to(keep[None], (S // 16, 16, 256)).reshape(S, 256)
            q = q_ref[:, window] * keep
            g = g_ref[:, window] * keep
            k = k_ref[:, window]
            v = v_ref[:, window]
            scores = mm(k, q, NT) * scale - log_ref[pl.ds(h, 1), :]
            if masked:
                scores = scores + bias[...]
            probs = jnp.exp(scores)
            dscore = (probs * (mm(v, g, NT) - center_ref[pl.ds(h, 1), :]) * scale).astype(BF16)
            out[0, :, window] = out[0, :, window] + mm(dscore, k * keep, TN).astype(BF16)
            out[1, :, window] = out[1, :, window] + mm(dscore, q, NN).astype(BF16)
            out[2, :, window] = out[2, :, window] + mm(probs.astype(BF16), g, NN).astype(BF16)
            return carry

        lax.fori_loop(first, end, one, 0)

    own_rest.wait()
    own_back = []
    for n, ((first, end), (begin, stop), (low, top)) in enumerate(zip(GROUPS, FORWARD, BACK)):
        drain(R.at[1:4, 0:others, begin:stop], a_r.at[1 + n])
        heads(first, end, R.at[1], R.at[2], R.at[3], GT, tlog, cent, True, TD)
        columns = pl.ds(low, top - low)

        def send_back(k, carry, n=n, columns=columns):
            d = seq_peer(k)
            remote(TD.at[:, rows_of(d), columns], TE.at[:, row_me, columns], b_s.at[n], b_r.at[n], seq=d).start()
            return carry

        lax.fori_loop(1, SEQ, send_back, 0)
        back = pltpu.make_async_copy(TD.at[:, row_me, columns], TE.at[:, row_me, columns], own_sem.at[3 + n])
        back.start()
        own_back.append(back)

    drain(prec.at[0], pp_r.at[0])
    for k in range(1, YS):
        drain(yrecv.at[k - 1], y_r.at[k - 1])
    for n in range(D // 128):
        columns = slice(128 * n, 128 * (n + 1))
        held = mine[0, :, columns] + prec[0, :, columns].astype(F32)
        for k in range(YS - 1):
            held = held + yrecv[k, :, columns].astype(F32)
        held = jnp.concatenate((held, jnp.zeros((WIDE - YROWS, 128), F32)), axis=0)
        xzsend[128 * n:128 * (n + 1), :] = held.T.astype(BF16)
    for k in range(1, CHIPS):
        there = pl.ds(pl.multiple_of(lax.rem(chip + k, CHIPS) * CHIP_ROWS, 16), CHIP_ROWS)
        remote(xzsend.at[there], xzrecv.at[k - 1], xz_s, xz_r, seq=chip_peer(k)).start()

    stage3(1)
    total = jnp.zeros((128, S), F32)
    for n in range(D // WIDE):
        columns = slice(n * WIDE, (n + 1) * WIDE)
        grad = project(X[0], 1, n)
        GS[:, columns] = grad
        high, low = split(grad, O[0, :, columns])
        total = total + (mm(ind[:, columns], high, NT) + mm(ind[:, columns], low, NT))
    cens[...] = total
    for n in (6, 7, 8):
        loads[n].wait()
    heads(0, HEADS, SI.at[0], SI.at[1], SI.at[2], GS, slog, cens, False, SD)
    writes = [
        pltpu.make_async_copy(SD.at[n], ref, out_sem.at[n]) for n, ref in enumerate((osq, osk, osv))
    ]
    for write in writes:
        write.start()

    drain(xzrecv, xz_r)
    held = xzsend[chip_rows, :].astype(F32)
    for k in range(CHIPS - 1):
        held = held + xzrecv[k].astype(F32)
    for i in range(ZHS):
        moved = pltpu.roll(held, WIDE - HEAD * i, axis=1) if i else held
        for c in range(2):
            zs[2 * i + c] = moved[HEAD * c:HEAD * (c + 1), 0:128]
    slot = core * ZHS + zh
    for k in range(1, 2 * ZHS):
        to_zh, to_core = z_peer(k)
        remote(
            zs.at[2 * to_zh + to_core], zr.at[slot], z_s, z_r, clip=to_zh * YS + y, seq=2 * chip + to_core
        ).start()
    zr[slot] = zs[corner]

    for n, (low, top) in enumerate(BACK):
        own_back[n].wait()
        drain(TE.at[:, 0:others, low:top], b_r.at[n])
    for n, ref in enumerate((otq, otk, otv)):
        write = pltpu.make_async_copy(TE.at[n], ref, out_sem.at[3 + n])
        write.start()
        writes.append(write)

    drain(zr.at[0:2 * ZHS - 1], z_r)
    ows[...] = (zr[0] + zr[1] + zr[2] + zr[3])[:, 0:HEAD]
    owt[...] = (zr[4] + zr[5] + zr[6] + zr[7])[:, 0:HEAD]

    drain(X.at[0, 0:others], a_s.at[0])
    for n, (begin, stop) in enumerate(FORWARD):
        drain(X.at[1:4, 0:others, begin:stop], a_s.at[1 + n])
    for n, (low, top) in enumerate(BACK):
        drain(TD.at[:, 0:others, low:top], b_s.at[n])
    for m in range(2):
        drain(W.at[m, 0:(CHIPS - 1) * CHIP_ROWS, 0:128], w1_s.at[m])
        drain(W.at[m, :, 0:384], w2_s.at[m])
        drain(W.at[m, :, 0:512], w3_s.at[m])
    drain(W.at[0, 0:(CHIPS - 1) * CHIP_ROWS, 0:128], lf_s)
    drain(W.at[0, :, 0:128], l3_s)
    drain(cen.at[0:others], c_s)
    for k in range(YS):
        drain(psend.at[k], pp_s.at[k])
    for k in range(YS - 1):
        drain(ysend.at[k], y_s.at[k])
    drain(xzsend.at[0:(CHIPS - 1) * CHIP_ROWS], xz_s)
    drain(zs.at[0:2 * ZHS - 1], z_s)
    for write in writes:
        write.wait()


def shards(
    space_query, space_keys, space_values, space_output, space_logsum,
    time_query, time_keys, time_values, time_output, time_logsum,
    upstream, space_weight, time_weight,
):
    flat = (S, D)
    time_log = time_logsum.reshape(POS, HEADS, SEQ).transpose(1, 2, 0).reshape(HEADS, S)
    dma = pltpu.SemaphoreType.DMA
    big = jax.ShapeDtypeStruct(flat, BF16)
    small = jax.ShapeDtypeStruct((HEAD, HEAD), F32)
    anywhere = pl.BlockSpec(memory_space=pl.ANY)
    held = pl.BlockSpec(memory_space=pltpu.VMEM)
    results = pl.pallas_call(
        kernel,
        out_shape=(big,) * 6 + (small,) * 2,
        in_specs=[anywhere] * 9 + [held] * 4,
        out_specs=(anywhere,) * 6 + (held,) * 2,
        scratch_shapes=[
            pltpu.VMEM((4, S, D), BF16),
            pltpu.VMEM((4, S, D), BF16),
            pltpu.VMEM((2, S, D), BF16),
            pltpu.VMEM((3, S, D), BF16),
            pltpu.VMEM((S, D), BF16),
            pltpu.VMEM((S, D), BF16),
            pltpu.VMEM((3, S, D), BF16),
            pltpu.VMEM((3, S, D), BF16),
            pltpu.VMEM((3, S, D), BF16),
            pltpu.VMEM((2, D, D), BF16),
            pltpu.VMEM((2, CHIP_ROWS, D), BF16),
            pltpu.VMEM((2, HEAD, D), F32),
            pltpu.VMEM((2, HEAD, D), F32),
            pltpu.VMEM((128, D), BF16),
            pltpu.VMEM((S, S), F32),
            pltpu.VMEM((S, 128), F32),
            pltpu.VMEM((S, 128), F32),
            pltpu.VMEM((128, S), F32),
            pltpu.VMEM((128, S), F32),
            pltpu.VMEM((D, S), F32),
            pltpu.VMEM((YS, YROWS, S), BF16),
            pltpu.VMEM((YS, YROWS, D), F32),
            pltpu.VMEM((YS, YROWS, D), BF16),
            pltpu.VMEM((YS, YROWS, D), BF16),
            pltpu.VMEM((YS - 1, YROWS, D), BF16),
            pltpu.VMEM((YS - 1, YROWS, D), BF16),
            pltpu.VMEM((D, WIDE), BF16),
            pltpu.VMEM((CHIPS - 1, CHIP_ROWS, WIDE), BF16),
            pltpu.VMEM((2 * ZHS, HEAD, 128), F32),
            pltpu.VMEM((2 * ZHS, HEAD, 128), F32),
            dma((9,)), dma((6,)), dma, dma, dma((2,)), dma((2,)), dma, dma,
            dma((2,)), dma((2,)), dma((2,)), dma((2,)), dma, dma,
            dma((4,)), dma((4,)), dma, dma, dma((3,)), dma((3,)), dma((4,)), dma((4,)),
            dma((3,)), dma((3,)), dma, dma, dma, dma, dma((6,)),
        ],
        compiler_params=pltpu.CompilerParams(
            collective_id=0, has_side_effects=True, vmem_limit_bytes=60 * 1024 * 1024
        ),
        cost_estimate=pl.CostEstimate(flops=7_000_000_000, bytes_accessed=12_000_000, transcendentals=2_100_000),
    )(
        upstream.reshape(flat), time_query.reshape(flat), time_keys.reshape(flat), time_values.reshape(flat),
        space_output.reshape(flat), time_output.reshape(flat),
        space_query.reshape(flat), space_keys.reshape(flat), space_values.reshape(flat),
        space_weight, time_weight, space_logsum.reshape(HEADS, S), time_log,
    )
    local = (1, 1, S, D)
    return tuple(result.reshape(local) for result in results[:6]) + tuple(results[6:])


def solution(mesh):
    block = P("clip", "seq", None, None)
    return jax.shard_map(
        shards,
        mesh=mesh,
        in_specs=(block,) * 11 + (P("seq", None),) * 2,
        out_specs=(block,) * 6 + (P("seq", "clip"),) * 2,
        check_vma=False,
    )
```

profile of v0, /device:TPU:1, one launch (start us, length us, event | category | flops | bytes accessed | tf_op | source)
XLA Modules:
  0.0 113.9 jit_solution(10274466555772779268)
XLA Ops:
  0.6 1.0 copy.21
  1.6 0.7 reshape.81.tlog
  2.4 102.2 %shard_map.188 = (bf16[256,1152]{1,0:T(8,128)(2,1)}, bf16[256,1152]{1,0:T(8,128)(2,1)}, bf16[256,1152]{1,0:T(8,128)(2,1)}, bf16[256,1152]{1,0:T(8,128)(2,1)}, bf...) custom-call(bf16[256,1152]{1,0:T(8,128)(2,1)} %bitcast.26, ...), custom_call_target="tpu_custom_call" | custom-call | flops 7000000000 | bytes 12000000 | tf_op jit(solution)/shard_map/pallas_call | solution.py:397
  104.5 0.0 copy-start.4
  104.5 2.0 %copy.30 = bf16[1,1,256,1152]{3,2,1,0:T(8,128)(2,1)} copy(bf16[1,1,256,1152]{3,2,1,0:T(8,128)(2,1)} %bitcast.24) | data formatting | bytes 1179648
  106.5 0.0 copy-done.4
  106.5 0.0 copy-start.3
  106.5 0.8 copy.31
  107.3 0.5 copy-done.3
  107.8 0.0 copy-start.2
  107.8 0.8 copy.32
  108.6 0.5 copy-done.2
  109.1 0.0 copy-start.1
  109.1 0.8 copy.33
  109.9 0.5 copy-done.1
  110.4 0.0 copy-start
  110.4 0.8 copy.34
  111.2 0.5 copy-done
  111.6 0.0 copy-start.6
  111.6 0.8 copy.35
  112.5 0.0 copy-done.6
  112.5 0.0 copy-start.5
  112.5 0.6 copy.36
  113.1 0.2 copy-done.5
  113.2 0.6 copy.37
Async XLA Ops:
  104.5 2.0 %copy-start.4 = (bf16[256,1152]{1,0:T(8,128)(2,1)S(1)}, bf16[256,1152]{1,0:T(8,128)(2,1)}, u32[]{:S(2)}) copy-start(bf16[256,1152]{1,0:T(8,128)(2,1)} %get-tuple-element.17) | copy-start | bytes 1769476
  106.5 1.3 %copy-start.3 = (bf16[256,1152]{1,0:T(8,128)(2,1)S(1)}, bf16[256,1152]{1,0:T(8,128)(2,1)}, u32[]{:S(2)}) copy-start(bf16[256,1152]{1,0:T(8,128)(2,1)} %get-tuple-element.18) | copy-start | bytes 1769476
  107.8 1.3 %copy-start.2 = (bf16[256,1152]{1,0:T(8,128)(2,1)S(1)}, bf16[256,1152]{1,0:T(8,128)(2,1)}, u32[]{:S(2)}) copy-start(bf16[256,1152]{1,0:T(8,128)(2,1)} %get-tuple-element.19) | copy-start | bytes 1769476
  109.1 1.3 %copy-start.1 = (bf16[256,1152]{1,0:T(8,128)(2,1)S(1)}, bf16[256,1152]{1,0:T(8,128)(2,1)}, u32[]{:S(2)}) copy-start(bf16[256,1152]{1,0:T(8,128)(2,1)} %get-tuple-element.20) | copy-start | bytes 1769476
  110.4 1.3 %copy-start = (bf16[256,1152]{1,0:T(8,128)(2,1)S(1)}, bf16[256,1152]{1,0:T(8,128)(2,1)}, u32[]{:S(2)}) copy-start(bf16[256,1152]{1,0:T(8,128)(2,1)} %get-tuple-element.21) | copy-start | bytes 1769476
  111.6 0.8 copy-start.6
  112.5 0.8 copy-start.5
where the time goes:
time: 115 us; the launch traced here: 114 us
  Pallas kernels  102 us (89%)
  local copies, waits for them, and re-layouts  11 us (10%)
    pallas_call x1, Pallas kernels, shards(): pl.pallas_call(kernel, out_shape=(big,) * 6 + (small,) * 2, in_specs=[any...  102 us
    unnamed x22, local copies, waits for them, and re-layouts  9.31 us

commit v1 on v0

--- a/solution.py
+++ b/solution.py
@@ -21,6 +21,7 @@
 CHIP_ROWS = 2 * HEAD
 YROWS = ZHS * HEAD
 WIDE = 384
+ZROWS = 80
 GROUPS = ((0, 6), (6, 11), (11, 16))
 FORWARD = ((0, 512), (512, 896), (896, 1152))
 BACK = ((0, 384), (384, 768), (768, 1152))
@@ -36,11 +37,11 @@
 def kernel(
     up, tq, tk, tv, so, to, sq, sk, sv, ws, wt, slog, tlog,
     osq, osk, osv, otq, otk, otv, ows, owt,
-    X, R, O, SI, GT, GS, TD, TE, SD, W, wown, w32, w32r,
+    X, R, O, SI, GT, GS, TD, TE, W, wown, w32, w32r,
     ind, bias, cen, cenr, cent, cens,
-    ut, utp, mine, psend, prec, ysend, yrecv, xzsend, xzrecv, zs, zr,
-    ld, own_sem, wp_s, wp_r, w1_s, w1_r, lf_s, lf_r, w2_s, w2_r, w3_s, w3_r, l3_s, l3_r,
-    a_s, a_r, c_s, c_r, b_s, b_r, pp_s, pp_r, y_s, y_r, xz_s, xz_r, z_s, z_r, out_sem,
+    ut, utp, mine, psend, prec, ysend, yfar, yrecv, xzsend, xzrecv, zs, zr,
+    ld, own_sem, wp_s, wp_r, w1_s, w1_r, lf_s, lf_r, w2_s, w2_r, wf_s, wf_r, w3_s, w3_r, l3_s, l3_r,
+    a_s, a_r, c_s, c_r, b_s, b_r, pp_s, pp_r, yf_s, yf_r, y_s, y_r, xz_s, xz_r, z_s, z_r, out_sem,
 ):
     clip = lax.axis_index("clip")
     seq = lax.axis_index("seq")
@@ -76,7 +77,7 @@
     barrier = pltpu.get_barrier_semaphore()
     for k in range(1, SEQ):
         pl.semaphore_signal(barrier, inc=1, device_id={"seq": seq_peer(k)}, device_id_type=pl.DeviceIdType.MESH)
-    for k in range(1, YS):
+    for k in (1, YS - 1):
         pl.semaphore_signal(barrier, inc=1, device_id={"clip": y_peer(k)}, device_id_type=pl.DeviceIdType.MESH)
     for k in range(1, 2 * ZHS):
         to_zh, to_core = z_peer(k)
@@ -97,7 +98,19 @@
     w32[0] = wt[...].astype(F32)
     w32[1] = ws[...].astype(F32)
 
-    pl.semaphore_wait(barrier, (SEQ - 1) + (YS - 1) + (2 * ZHS - 1))
+    head_row = lax.broadcasted_iota(jnp.int32, (128, D), 0) * HEAD
+    column = lax.broadcasted_iota(jnp.int32, (128, D), 1)
+    ind[...] = jnp.where((column >= head_row) & (column < head_row + HEAD), 1.0, 0.0).astype(BF16)
+    zeros = jnp.zeros((S, D), BF16)
+    for n in range(3):
+        TD[n] = zeros
+    for ref in (osq, osk, osv):
+        ref[...] = zeros
+    position = lax.broadcasted_iota(jnp.int32, (S, S), 0)
+    other = lax.broadcasted_iota(jnp.int32, (S, S), 1)
+    bias[...] = jnp.where(lax.rem(position, POS) == lax.rem(other, POS), 0.0, -1e30)
+
+    pl.semaphore_wait(barrier, (SEQ - 1) + 2 + (2 * ZHS - 1))
 
     pair = remote(w32, w32r, wp_s, wp_r, seq=sibling)
     pair.start()
@@ -113,14 +126,10 @@
         remote(X.at[0, rows_of(d)], R.at[0, row_me], a_s.at[0], a_r.at[0], seq=d).start()
         return carry
 
-    lax.fori_loop(1, SEQ, send_up, 0)
     own_up = pltpu.make_async_copy(X.at[0, row_me], R.at[0, row_me], own_sem.at[0])
     own_up.start()
-
-    head_row = lax.broadcasted_iota(jnp.int32, (128, D), 0) * HEAD
-    column = lax.broadcasted_iota(jnp.int32, (128, D), 1)
-    ind[...] = jnp.where((column >= head_row) & (column < head_row + HEAD), 1.0, 0.0).astype(BF16)
-
+    for n in range(D // 128):
+        ut[128 * n:128 * (n + 1), :] = X[0, :, 128 * n:128 * (n + 1)].astype(F32).T
     pair.wait()
     chip_rows = pl.ds(pl.multiple_of(chip * CHIP_ROWS, 16), CHIP_ROWS)
     tile = pl.ds(pl.multiple_of((2 * y + core) * 128, 128), 128)
@@ -147,26 +156,8 @@
         return carry
 
     lax.fori_loop(1, CHIPS, send_last, 0)
-
-    for n in (1, 2, 3):
-        loads[n].wait()
-    for g, (begin, end) in enumerate(FORWARD):
-        columns = pl.ds(begin, end - begin)
-
-        def send_group(k, carry, g=g, columns=columns):
-            d = seq_peer(k)
-            remote(
-                X.at[1:4, rows_of(d), columns], R.at[1:4, row_me, columns], a_s.at[1 + g], a_r.at[1 + g], seq=d
-            ).start()
-            return carry
-
-        lax.fori_loop(1, SEQ, send_group, 0)
-    own_rest = pltpu.make_async_copy(X.at[1:4, row_me], R.at[1:4, row_me], own_sem.at[1])
-    own_rest.start()
-    stage1(1)
-
-    for n in range(D // 128):
-        ut[128 * n:128 * (n + 1), :] = X[0, :, 128 * n:128 * (n + 1)].astype(F32).T
+    lax.fori_loop(1, SEQ, send_up, 0)
+
     for j in range(YS):
         utp[j] = jnp.concatenate(
             [ut[HEAD * (YS * i + j):HEAD * (YS * i + j + 1), :] for i in range(ZHS)], axis=0
@@ -187,39 +178,87 @@
         lax.fori_loop(0, D // WIDE, piece, 0)
         remote(psend.at[k], prec.at[k], pp_s.at[k], pp_r.at[k], seq=sibling).start()
 
+    def tile_of(k):
+        return pl.ds(pl.multiple_of((2 * lax.rem(y + k, YS) + core) * 128, 128), 128)
+
+    def to_sibling(m, k):
+        remote(W.at[m, :, tile_of(k)], W.at[m, :, tile_of(k)], w3_s.at[m], w3_r.at[m], seq=sibling).start()
+
     def stage2(m):
         drain(W.at[m, 0:(CHIPS - 1) * CHIP_ROWS, 0:128], w1_r.at[m])
-        remote(W.at[m, :, tile], W.at[m, :, tile], w3_s.at[m], w3_r.at[m], seq=sibling).start()
-        for k in range(1, YS):
-            remote(W.at[m, :, tile], W.at[m, :, tile], w2_s.at[m], w2_r.at[m], clip=y_peer(k)).start()
+        for n, k in enumerate((1, YS - 1)):
+            remote(W.at[m, :, tile], W.at[m, :, tile], w2_s.at[m], w2_r.at[m, n], clip=y_peer(k)).start()
+        to_sibling(m, 0)
+
+    def forward2(m):
+        for n, k in enumerate((1, YS - 1)):
+            drain(W.at[m, :, 0:128], w2_r.at[m, n])
+            half = pl.ds(n * (D // 2), D // 2)
+            remote(
+                W.at[m, half, tile_of(YS - k)], W.at[m, half, tile_of(YS - k)], wf_s.at[m], wf_r.at[m], clip=y_peer(k)
+            ).start()
+            to_sibling(m, YS - k)
 
     def stage3(m):
-        drain(W.at[m, :, 0:384], w2_r.at[m])
-        for k in range(1, YS):
-            there = pl.ds(pl.multiple_of((2 * lax.rem(y + k, YS) + core) * 128, 128), 128)
-            remote(W.at[m, :, there], W.at[m, :, there], w3_s.at[m], w3_r.at[m], seq=sibling).start()
+        drain(W.at[m, :, 0:128], wf_r.at[m])
+        to_sibling(m, 2)
         drain(W.at[m, :, 0:512], w3_r.at[m])
+
+    near = ((0, 1, 0, YROWS // 2), (1, YS - 1, YROWS // 2, YROWS))
+
+    def far_chunk():
+        drain(prec.at[2], pp_r.at[2])
+        ysend[1] = (mine[2] + prec[2].astype(F32)).astype(BF16)
+        for n, k, low, top in near:
+            remote(ysend.at[1, low:top], yfar.at[n], yf_s.at[n], yf_r.at[n], clip=y_peer(k)).start()
+
+    def near_first():
+        for n, k, low, top in near:
+            rows = slice(YROWS // 2 - low, YROWS // 2 - low + YROWS // 2)
+            drain(prec.at[k], pp_r.at[k])
+            ysend[k - 1, rows] = (mine[k, rows] + prec[k, rows].astype(F32)).astype(BF16)
+            remote(
+                ysend.at[k - 1, rows], yrecv.at[n, rows], y_s.at[0, n], y_r.at[0, n], clip=y_peer(k)
+            ).start()
+
+    def near_second():
+        for n, k, low, top in near:
+            rows = slice(low, top)
+            drain(yfar.at[n], yf_r.at[n])
+            ysend[k - 1, rows] = (
+                mine[k, rows] + prec[k, rows].astype(F32) + yfar[n].astype(F32)
+            ).astype(BF16)
+            remote(
+                ysend.at[k - 1, rows], yrecv.at[n, rows], y_s.at[1, n], y_r.at[1, n], clip=y_peer(k)
+            ).start()
 
     gradient(2)
     stage2(0)
     drain(W.at[0, 0:(CHIPS - 1) * CHIP_ROWS, 0:128], lf_r)
     remote(W.at[core, :, last], W.at[core, :, last], l3_s, l3_r, seq=sibling).start()
+    for n in (1, 2, 3):
+        loads[n].wait()
+    for g, (begin, end) in enumerate(FORWARD):
+        columns = pl.ds(begin, end - begin)
+
+        def send_group(k, carry, g=g, columns=columns):
+            d = seq_peer(k)
+            remote(
+                X.at[1:4, rows_of(d), columns], R.at[1:4, row_me, columns], a_s.at[1 + g], a_r.at[1 + g], seq=d
+            ).start()
+            return carry
+
+        lax.fori_loop(1, SEQ, send_group, 0)
+    own_rest = pltpu.make_async_copy(X.at[1:4, row_me], R.at[1:4, row_me], own_sem.at[1])
+    own_rest.start()
+
     gradient(1)
+    far_chunk()
+    forward2(0)
+    stage1(1)
     gradient(3)
-    for k in (2, 1, 3):
-        drain(prec.at[k], pp_r.at[k])
-        ysend[k - 1] = (mine[k] + prec[k].astype(F32)).astype(BF16)
-        remote(ysend.at[k - 1], yrecv.at[k - 1], y_s.at[k - 1], y_r.at[k - 1], clip=y_peer(k)).start()
+    near_first()
     gradient(0)
-    stage2(1)
-
-    zeros = jnp.zeros((S, D), BF16)
-    for n in range(3):
-        TD[n] = zeros
-        SD[n] = zeros
-    position = lax.broadcasted_iota(jnp.int32, (S, S), 0)
-    other = lax.broadcasted_iota(jnp.int32, (S, S), 1)
-    bias[...] = jnp.where(lax.rem(position, POS) == lax.rem(other, POS), 0.0, -1e30)
 
     stage3(0)
     drain(W.at[0, :, last], l3_r)
@@ -248,6 +287,7 @@
     own_cen = pltpu.make_async_copy(cen.at[row_me], cenr.at[row_me], own_sem.at[2])
     own_cen.start()
 
+    near_second()
     others = (SEQ - 1) * POS
     own_up.wait()
     drain(R.at[0, 0:others], a_r.at[0])
@@ -276,18 +316,34 @@
                 scores = scores + bias[...]
             probs = jnp.exp(scores)
             dscore = (probs * (mm(v, g, NT) - center_ref[pl.ds(h, 1), :]) * scale).astype(BF16)
-            out[0, :, window] = out[0, :, window] + mm(dscore, k * keep, TN).astype(BF16)
-            out[1, :, window] = out[1, :, window] + mm(dscore, q, NN).astype(BF16)
-            out[2, :, window] = out[2, :, window] + mm(probs.astype(BF16), g, NN).astype(BF16)
+            out[0][:, window] = out[0][:, window] + mm(dscore, k * keep, TN).astype(BF16)
+            out[1][:, window] = out[1][:, window] + mm(dscore, q, NN).astype(BF16)
+            out[2][:, window] = out[2][:, window] + mm(probs.astype(BF16), g, NN).astype(BF16)
             return carry
 
         lax.fori_loop(first, end, one, 0)
+
+    def over_chips():
+        drain(prec.at[0], pp_r.at[0])
+        for n in range(2):
+            for half in range(2):
+                drain(yrecv.at[n, 0:YROWS // 2], y_r.at[half, n])
+        for n in range(D // 128):
+            columns = slice(128 * n, 128 * (n + 1))
+            held = mine[0, :, columns] + prec[0, :, columns].astype(F32)
+            for n_from in range(2):
+                held = held + yrecv[n_from, :, columns].astype(F32)
+            held = jnp.concatenate((held, jnp.zeros((WIDE - YROWS, 128), F32)), axis=0)
+            xzsend[128 * n:128 * (n + 1), :] = held.T.astype(BF16)
+        for k in range(1, CHIPS):
+            there = pl.ds(pl.multiple_of(lax.rem(chip + k, CHIPS) * CHIP_ROWS, 16), CHIP_ROWS)
+            remote(xzsend.at[there], xzrecv.at[k - 1], xz_s, xz_r, seq=chip_peer(k)).start()
 
     own_rest.wait()
     own_back = []
     for n, ((first, end), (begin, stop), (low, top)) in enumerate(zip(GROUPS, FORWARD, BACK)):
         drain(R.at[1:4, 0:others, begin:stop], a_r.at[1 + n])
-        heads(first, end, R.at[1], R.at[2], R.at[3], GT, tlog, cent, True, TD)
+        heads(first, end, R.at[1], R.at[2], R.at[3], GT, tlog, cent, True, [TD.at[m] for m in range(3)])
         columns = pl.ds(low, top - low)
 
         def send_back(k, carry, n=n, columns=columns):
@@ -299,20 +355,11 @@
         back = pltpu.make_async_copy(TD.at[:, row_me, columns], TE.at[:, row_me, columns], own_sem.at[3 + n])
         back.start()
         own_back.append(back)
-
-    drain(prec.at[0], pp_r.at[0])
-    for k in range(1, YS):
-        drain(yrecv.at[k - 1], y_r.at[k - 1])
-    for n in range(D // 128):
-        columns = slice(128 * n, 128 * (n + 1))
-        held = mine[0, :, columns] + prec[0, :, columns].astype(F32)
-        for k in range(YS - 1):
-            held = held + yrecv[k, :, columns].astype(F32)
-        held = jnp.concatenate((held, jnp.zeros((WIDE - YROWS, 128), F32)), axis=0)
-        xzsend[128 * n:128 * (n + 1), :] = held.T.astype(BF16)
-    for k in range(1, CHIPS):
-        there = pl.ds(pl.multiple_of(lax.rem(chip + k, CHIPS) * CHIP_ROWS, 16), CHIP_ROWS)
-        remote(xzsend.at[there], xzrecv.at[k - 1], xz_s, xz_r, seq=chip_peer(k)).start()
+        if n == 0:
+            stage2(1)
+        elif n == 1:
+            over_chips()
+            forward2(1)
 
     stage3(1)
     total = jnp.zeros((128, S), F32)
@@ -325,12 +372,8 @@
     cens[...] = total
     for n in (6, 7, 8):
         loads[n].wait()
-    heads(0, HEADS, SI.at[0], SI.at[1], SI.at[2], GS, slog, cens, False, SD)
-    writes = [
-        pltpu.make_async_copy(SD.at[n], ref, out_sem.at[n]) for n, ref in enumerate((osq, osk, osv))
-    ]
-    for write in writes:
-        write.start()
+    spatial = (SI.at[0], SI.at[1], SI.at[2], GS, slog, cens, False, (osq, osk, osv))
+    heads(0, HEADS // 2, *spatial)
 
     drain(xzrecv, xz_r)
     held = xzsend[chip_rows, :].astype(F32)
@@ -339,7 +382,8 @@
     for i in range(ZHS):
         moved = pltpu.roll(held, WIDE - HEAD * i, axis=1) if i else held
         for c in range(2):
-            zs[2 * i + c] = moved[HEAD * c:HEAD * (c + 1), 0:128]
+            part = jnp.concatenate((moved[HEAD * c:HEAD * (c + 1), 0:128], jnp.zeros((ZROWS - HEAD, 128), F32)), axis=0)
+            zs[2 * i + c] = part.astype(BF16)
     slot = core * ZHS + zh
     for k in range(1, 2 * ZHS):
         to_zh, to_core = z_peer(k)
@@ -347,18 +391,21 @@
             zs.at[2 * to_zh + to_core], zr.at[slot], z_s, z_r, clip=to_zh * YS + y, seq=2 * chip + to_core
         ).start()
     zr[slot] = zs[corner]
-
+    heads(HEADS // 2, HEADS, *spatial)
+
+    writes = []
     for n, (low, top) in enumerate(BACK):
         own_back[n].wait()
         drain(TE.at[:, 0:others, low:top], b_r.at[n])
     for n, ref in enumerate((otq, otk, otv)):
-        write = pltpu.make_async_copy(TE.at[n], ref, out_sem.at[3 + n])
+        write = pltpu.make_async_copy(TE.at[n], ref, out_sem.at[n])
         write.start()
         writes.append(write)
 
     drain(zr.at[0:2 * ZHS - 1], z_r)
-    ows[...] = (zr[0] + zr[1] + zr[2] + zr[3])[:, 0:HEAD]
-    owt[...] = (zr[4] + zr[5] + zr[6] + zr[7])[:, 0:HEAD]
+    for m, ref in enumerate((ows, owt)):
+        four = [zr[ZHS * m + i].astype(F32) for i in range(ZHS)]
+        ref[...] = (four[0] + four[1] + four[2] + four[3])[0:HEAD, 0:HEAD]
 
     drain(X.at[0, 0:others], a_s.at[0])
     for n, (begin, stop) in enumerate(FORWARD):
@@ -367,19 +414,37 @@
         drain(TD.at[:, 0:others, low:top], b_s.at[n])
     for m in range(2):
         drain(W.at[m, 0:(CHIPS - 1) * CHIP_ROWS, 0:128], w1_s.at[m])
-        drain(W.at[m, :, 0:384], w2_s.at[m])
+        drain(W.at[m, :, 0:256], w2_s.at[m])
+        drain(W.at[m, :, 0:128], wf_s.at[m])
         drain(W.at[m, :, 0:512], w3_s.at[m])
     drain(W.at[0, 0:(CHIPS - 1) * CHIP_ROWS, 0:128], lf_s)
     drain(W.at[0, :, 0:128], l3_s)
     drain(cen.at[0:others], c_s)
     for k in range(YS):
         drain(psend.at[k], pp_s.at[k])
-    for k in range(YS - 1):
-        drain(ysend.at[k], y_s.at[k])
+    for n in range(2):
+        drain(yfar.at[n], yf_s.at[n])
+        for half in range(2):
+            drain(yfar.at[n], y_s.at[half, n])
     drain(xzsend.at[0:(CHIPS - 1) * CHIP_ROWS], xz_s)
     drain(zs.at[0:2 * ZHS - 1], z_s)
     for write in writes:
         write.wait()
+
+
+def write_out(*refs):
+    count = len(refs) // 2 - 2
+    sources, targets, sem = refs[:count + 2], refs[count + 2:-1], refs[-1]
+    copies = [
+        pltpu.make_async_copy(src, dst, sem.at[n])
+        for n, (src, dst) in enumerate(zip(sources[:count], targets[:count]))
+    ]
+    for copy in copies:
+        copy.start()
+    for src, dst in zip(sources[count:], targets[count:]):
+        dst[...] = src[...]
+    for copy in copies:
+        copy.wait()
 
 
 def shards(
@@ -396,9 +461,8 @@
     held = pl.BlockSpec(memory_space=pltpu.VMEM)
     results = pl.pallas_call(
         kernel,
-        out_shape=(big,) * 6 + (small,) * 2,
+        out_shape=(pltpu.VMEM(flat, BF16),) * 6 + (pltpu.VMEM((HEAD, HEAD), F32),) * 2,
         in_specs=[anywhere] * 9 + [held] * 4,
-        out_specs=(anywhere,) * 6 + (held,) * 2,
         scratch_shapes=[
             pltpu.VMEM((4, S, D), BF16),
             pltpu.VMEM((4, S, D), BF16),
@@ -406,7 +470,6 @@
             pltpu.VMEM((3, S, D), BF16),
             pltpu.VMEM((S, D), BF16),
             pltpu.VMEM((S, D), BF16),
-            pltpu.VMEM((3, S, D), BF16),
             pltpu.VMEM((3, S, D), BF16),
             pltpu.VMEM((3, S, D), BF16),
             pltpu.VMEM((2, D, D), BF16),
@@ -425,18 +488,19 @@
             pltpu.VMEM((YS, YROWS, D), BF16),
             pltpu.VMEM((YS, YROWS, D), BF16),
             pltpu.VMEM((YS - 1, YROWS, D), BF16),
-            pltpu.VMEM((YS - 1, YROWS, D), BF16),
+            pltpu.VMEM((2, YROWS // 2, D), BF16),
+            pltpu.VMEM((2, YROWS, D), BF16),
             pltpu.VMEM((D, WIDE), BF16),
             pltpu.VMEM((CHIPS - 1, CHIP_ROWS, WIDE), BF16),
-            pltpu.VMEM((2 * ZHS, HEAD, 128), F32),
-            pltpu.VMEM((2 * ZHS, HEAD, 128), F32),
+            pltpu.VMEM((2 * ZHS, ZROWS, 128), BF16),
+            pltpu.VMEM((2 * ZHS, ZROWS, 128), BF16),
             dma((9,)), dma((6,)), dma, dma, dma((2,)), dma((2,)), dma, dma,
-            dma((2,)), dma((2,)), dma((2,)), dma((2,)), dma, dma,
+            dma((2,)), dma((2, 2)), dma((2,)), dma((2,)), dma((2,)), dma((2,)), dma, dma,
             dma((4,)), dma((4,)), dma, dma, dma((3,)), dma((3,)), dma((4,)), dma((4,)),
-            dma((3,)), dma((3,)), dma, dma, dma, dma, dma((6,)),
+            dma((2,)), dma((2,)), dma((2, 2)), dma((2, 2)), dma, dma, dma, dma, dma((3,)),
         ],
         compiler_params=pltpu.CompilerParams(
-            collective_id=0, has_side_effects=True, vmem_limit_bytes=60 * 1024 * 1024
+            collective_id=0, has_side_effects=True, vmem_limit_bytes=60 * 1024 * 1024 - 256 * 1024
         ),
         cost_estimate=pl.CostEstimate(flops=7_000_000_000, bytes_accessed=12_000_000, transcendentals=2_100_000),
     )(
@@ -445,6 +509,14 @@
         space_query.reshape(flat), space_keys.reshape(flat), space_values.reshape(flat),
         space_weight, time_weight, space_logsum.reshape(HEADS, S), time_log,
     )
+    results = pl.pallas_call(
+        write_out,
+        out_shape=(big,) * 6 + (small,) * 2,
+        in_specs=[anywhere] * 6 + [held] * 2,
+        out_specs=(anywhere,) * 6 + (held,) * 2,
+        scratch_shapes=[dma((6,))],
+        compiler_params=pltpu.CompilerParams(vmem_limit_bytes=1024 * 1024),
+    )(*results)
     local = (1, 1, S, D)
     return tuple(result.reshape(local) for result in results[:6]) + tuple(results[6:])
 

time: 115 us -> 96.8 us (0.84)
  local copies, waits for them, and re-layouts: 11 us -> 1.73 us
  Pallas kernels: 102 us -> 94.3 us
    unnamed x22 -> x0, local copies, waits for them, and re-layouts: 9.31 us -> none
    pallas_call x1 -> x2, Pallas kernels: 102 us -> 94.3 us  [the longest x1 91.9 us: shards(): pl.pallas_call(kernel, out_shape=(pltpu.VMEM(flat, BF16),) * 6 + (pltpu.V...]
where the time goes in v1:
time: 96.8 us; the launch traced here: 96.7 us
  Pallas kernels  94.3 us (97%)
  local copies, waits for them, and re-layouts  1.73 us (2%)
    pallas_call x1, Pallas kernels, shards(): pl.pallas_call(kernel, out_shape=(pltpu.VMEM(flat, BF16),) * 6 + (pltpu.V...  91.9 us
    pallas_call x1, Pallas kernels, shards(): pl.pallas_call(write_out, out_shape=(big,) * 6 + (small,) * 2, in_specs=[...  2.47 us

profile of v1, /device:TPU:1, one launch (start us, length us, event | category | flops | bytes accessed | tf_op | source)
XLA Modules:
  0.0 96.7 jit_solution(13975291294216801360)
XLA Ops:
  0.6 1.0 %copy.21 = f32[16,16,16]{2,1,0:T(8,128)S(1)} copy(f32[16,16,16]{1,0,2:T(8,128)} %bitcast.19) | data formatting | bytes 32768 | tf_op jit(solution)/shard_map/transpose | solution.py:456
  1.6 0.7 reshape.81.tlog
  2.4 91.9 %shard_map.188 = (bf16[256,1152]{1,0:T(8,128)(2,1)S(1)}, bf16[256,1152]{1,0:T(8,128)(2,1)S(1)}, bf16[256,1152]{1,0:T(8,128)(2,1)S(1)}, bf16[256,1152]{1,0:T(8,12...) custom-call(bf16[256,1152]{1,0:T(8,128)(2,1)} %bitcast.20, ...), custom_call_target="tpu_custom_call" | custom-call | flops 7000000000 | bytes 12000000 | tf_op jit(solution)/shard_map/pallas_call | solution.py:462
  94.2 2.5 %shard_map.189 = (bf16[256,1152]{1,0:T(8,128)(2,1)}, bf16[256,1152]{1,0:T(8,128)(2,1)}, bf16[256,1152]{1,0:T(8,128)(2,1)}, bf16[256,1152]{1,0:T(8,128)(2,1)}, bf...) custom-call(bf16[256,1152]{1,0:T(8,128)(2,1)S(1)} %get-tuple-element.24.refs_0_, ...), custom_call_target="tpu_custom_call" | custom-call | tf_op jit(solution)/shard_map/pallas_call | solution.py:512

commit v2 on v1

--- a/solution.py
+++ b/solution.py
@@ -22,6 +22,7 @@
 YROWS = ZHS * HEAD
 WIDE = 384
 ZROWS = 80
+REST = CHIP_ROWS // 3
 GROUPS = ((0, 6), (6, 11), (11, 16))
 FORWARD = ((0, 512), (512, 896), (896, 1152))
 BACK = ((0, 384), (384, 768), (768, 1152))
@@ -38,10 +39,10 @@
     up, tq, tk, tv, so, to, sq, sk, sv, ws, wt, slog, tlog,
     osq, osk, osv, otq, otk, otv, ows, owt,
     X, R, O, SI, GT, GS, TD, TE, W, wown, w32, w32r,
-    ind, bias, cen, cenr, cent, cens,
-    ut, utp, mine, psend, prec, ysend, yfar, yrecv, xzsend, xzrecv, zs, zr,
+    ind, bias, tl, cen, cenr, cent, cens,
+    ut, utp, mine, psend, prec, ysend, yfar, yrecv, xzsend, xzrecv, rest, restrecv, zs, zr,
     ld, own_sem, wp_s, wp_r, w1_s, w1_r, lf_s, lf_r, w2_s, w2_r, wf_s, wf_r, w3_s, w3_r, l3_s, l3_r,
-    a_s, a_r, c_s, c_r, b_s, b_r, pp_s, pp_r, yf_s, yf_r, y_s, y_r, xz_s, xz_r, z_s, z_r, out_sem,
+    a_s, a_r, c_s, c_r, b_s, b_r, pp_s, pp_r, yf_s, yf_r, y_s, y_r, xz_s, xz_r, xr_s, xr_r, z_s, z_r, out_sem,
 ):
     clip = lax.axis_index("clip")
     seq = lax.axis_index("seq")
@@ -98,18 +99,6 @@
     w32[0] = wt[...].astype(F32)
     w32[1] = ws[...].astype(F32)
 
-    head_row = lax.broadcasted_iota(jnp.int32, (128, D), 0) * HEAD
-    column = lax.broadcasted_iota(jnp.int32, (128, D), 1)
-    ind[...] = jnp.where((column >= head_row) & (column < head_row + HEAD), 1.0, 0.0).astype(BF16)
-    zeros = jnp.zeros((S, D), BF16)
-    for n in range(3):
-        TD[n] = zeros
-    for ref in (osq, osk, osv):
-        ref[...] = zeros
-    position = lax.broadcasted_iota(jnp.int32, (S, S), 0)
-    other = lax.broadcasted_iota(jnp.int32, (S, S), 1)
-    bias[...] = jnp.where(lax.rem(position, POS) == lax.rem(other, POS), 0.0, -1e30)
-
     pl.semaphore_wait(barrier, (SEQ - 1) + 2 + (2 * ZHS - 1))
 
     pair = remote(w32, w32r, wp_s, wp_r, seq=sibling)
@@ -126,6 +115,7 @@
         remote(X.at[0, rows_of(d)], R.at[0, row_me], a_s.at[0], a_r.at[0], seq=d).start()
         return carry
 
+    lax.fori_loop(1, SEQ, send_up, 0)
     own_up = pltpu.make_async_copy(X.at[0, row_me], R.at[0, row_me], own_sem.at[0])
     own_up.start()
     for n in range(D // 128):
@@ -156,7 +146,28 @@
         return carry
 
     lax.fori_loop(1, CHIPS, send_last, 0)
-    lax.fori_loop(1, SEQ, send_up, 0)
+
+    head_row = lax.broadcasted_iota(jnp.int32, (128, D), 0) * HEAD
+    column = lax.broadcasted_iota(jnp.int32, (128, D), 1)
+    ind[...] = jnp.where((column >= head_row) & (column < head_row + HEAD), 1.0, 0.0).astype(BF16)
+    zeros = jnp.zeros((S, D), BF16)
+    for n in range(3):
+        TD[n] = zeros
+    for ref in (osq, osk, osv):
+        ref[...] = zeros
+    position = lax.broadcasted_iota(jnp.int32, (S, S), 0)
+    other = lax.broadcasted_iota(jnp.int32, (S, S), 1)
+    bias[...] = jnp.where(lax.rem(position, POS) == lax.rem(other, POS), 0.0, -1e30)
+
+    frame = lax.broadcasted_iota(jnp.int32, (SEQ, S), 0) * POS
+    place = lax.broadcasted_iota(jnp.int32, (SEQ, S), 1)
+    spread = jnp.zeros((HEADS, S), F32)
+    for p in range(POS):
+        spread = spread + lax.dot_general(
+            tlog[p], jnp.where(place == frame + p, 1.0, 0.0), NN,
+            precision=lax.Precision.HIGHEST, preferred_element_type=F32,
+        )
+    tl[...] = spread
 
     for j in range(YS):
         utp[j] = jnp.concatenate(
@@ -232,33 +243,36 @@
                 ysend.at[k - 1, rows], yrecv.at[n, rows], y_s.at[1, n], y_r.at[1, n], clip=y_peer(k)
             ).start()
 
+    def forward(g):
+        begin, end = FORWARD[g]
+        columns = pl.ds(begin, end - begin)
+
+        def send_group(k, carry):
+            d = seq_peer(k)
+            remote(
+                X.at[1:4, rows_of(d), columns], R.at[1:4, row_me, columns], a_s.at[1 + g], a_r.at[1 + g], seq=d
+            ).start()
+            return carry
+
+        lax.fori_loop(1, SEQ, send_group, 0)
+
     gradient(2)
+    gradient(1)
+    far_chunk()
     stage2(0)
     drain(W.at[0, 0:(CHIPS - 1) * CHIP_ROWS, 0:128], lf_r)
     remote(W.at[core, :, last], W.at[core, :, last], l3_s, l3_r, seq=sibling).start()
     for n in (1, 2, 3):
         loads[n].wait()
-    for g, (begin, end) in enumerate(FORWARD):
-        columns = pl.ds(begin, end - begin)
-
-        def send_group(k, carry, g=g, columns=columns):
-            d = seq_peer(k)
-            remote(
-                X.at[1:4, rows_of(d), columns], R.at[1:4, row_me, columns], a_s.at[1 + g], a_r.at[1 + g], seq=d
-            ).start()
-            return carry
-
-        lax.fori_loop(1, SEQ, send_group, 0)
+    forward(0)
+    stage1(1)
+    forward(1)
     own_rest = pltpu.make_async_copy(X.at[1:4, row_me], R.at[1:4, row_me], own_sem.at[1])
     own_rest.start()
-
-    gradient(1)
-    far_chunk()
+    gradient(3)
     forward2(0)
-    stage1(1)
-    gradient(3)
     near_first()
-    gradient(0)
+    near_second()
 
     stage3(0)
     drain(W.at[0, :, last], l3_r)
@@ -276,7 +290,8 @@
         columns = slice(n * WIDE, (n + 1) * WIDE)
         high, low = split(project(X[0], 0, n), O[1, :, columns])
         total = total + (mm(high, ind[:, columns], NT) + mm(low, ind[:, columns], NT))
-    cen[...] = total
+    high = total.astype(BF16).astype(F32)
+    cen[...] = (high + pltpu.roll(total - high, HEADS, axis=1)).astype(BF16)
 
     def send_center(k, carry):
         d = seq_peer(k)
@@ -286,16 +301,18 @@
     lax.fori_loop(1, SEQ, send_center, 0)
     own_cen = pltpu.make_async_copy(cen.at[row_me], cenr.at[row_me], own_sem.at[2])
     own_cen.start()
-
-    near_second()
+    forward(2)
+
     others = (SEQ - 1) * POS
     own_up.wait()
     drain(R.at[0, 0:others], a_r.at[0])
     for n in range(D // WIDE):
         GT[:, n * WIDE:(n + 1) * WIDE] = project(R[0], 0, n)
+    gradient(0)
     own_cen.wait()
     drain(cenr.at[0:others], c_r)
-    cent[...] = cenr[...].T
+    both = cenr[...].astype(F32)
+    cent[...] = (both + pltpu.roll(both, 128 - HEADS, axis=1)).T
 
     scale = 1.0 / math.sqrt(HEAD)
     lane = lax.broadcasted_iota(jnp.int32, (16, 256), 1)
@@ -335,15 +352,26 @@
                 held = held + yrecv[n_from, :, columns].astype(F32)
             held = jnp.concatenate((held, jnp.zeros((WIDE - YROWS, 128), F32)), axis=0)
             xzsend[128 * n:128 * (n + 1), :] = held.T.astype(BF16)
+        for c in range(CHIPS):
+            parts = [
+                xzsend[CHIP_ROWS * c + REST * g:CHIP_ROWS * c + REST * (g + 1), 256:WIDE].astype(F32)
+                for g in range(3)
+            ]
+            rest[REST * c:REST * (c + 1), :] = (
+                parts[0] + pltpu.roll(parts[1], 32, axis=1) + pltpu.roll(parts[2], 64, axis=1)
+            ).astype(BF16)
         for k in range(1, CHIPS):
-            there = pl.ds(pl.multiple_of(lax.rem(chip + k, CHIPS) * CHIP_ROWS, 16), CHIP_ROWS)
-            remote(xzsend.at[there], xzrecv.at[k - 1], xz_s, xz_r, seq=chip_peer(k)).start()
+            to_chip = lax.rem(chip + k, CHIPS)
+            there = pl.ds(pl.multiple_of(to_chip * CHIP_ROWS, 16), CHIP_ROWS)
+            remote(xzsend.at[there, 0:256], xzrecv.at[k - 1], xz_s, xz_r, seq=chip_peer(k)).start()
+            there = pl.ds(pl.multiple_of(to_chip * REST, 16), REST)
+            remote(rest.at[there], restrecv.at[k - 1], xr_s, xr_r, seq=chip_peer(k)).start()
 
     own_rest.wait()
     own_back = []
     for n, ((first, end), (begin, stop), (low, top)) in enumerate(zip(GROUPS, FORWARD, BACK)):
         drain(R.at[1:4, 0:others, begin:stop], a_r.at[1 + n])
-        heads(first, end, R.at[1], R.at[2], R.at[3], GT, tlog, cent, True, [TD.at[m] for m in range(3)])
+        heads(first, end, R.at[1], R.at[2], R.at[3], GT, tl, cent, True, [TD.at[m] for m in range(3)])
         columns = pl.ds(low, top - low)
 
         def send_back(k, carry, n=n, columns=columns):
@@ -356,9 +384,9 @@
         back.start()
         own_back.append(back)
         if n == 0:
+            over_chips()
             stage2(1)
         elif n == 1:
-            over_chips()
             forward2(1)
 
     stage3(1)
@@ -373,12 +401,15 @@
     for n in (6, 7, 8):
         loads[n].wait()
     spatial = (SI.at[0], SI.at[1], SI.at[2], GS, slog, cens, False, (osq, osk, osv))
-    heads(0, HEADS // 2, *spatial)
-
     drain(xzrecv, xz_r)
-    held = xzsend[chip_rows, :].astype(F32)
+    drain(restrecv, xr_r)
+    held = xzsend[chip_rows, 0:256].astype(F32)
+    side = rest[pl.ds(pl.multiple_of(chip * REST, 16), REST), :].astype(F32)
     for k in range(CHIPS - 1):
         held = held + xzrecv[k].astype(F32)
+        side = side + restrecv[k].astype(F32)
+    side = jnp.concatenate((side, pltpu.roll(side, 96, axis=1), pltpu.roll(side, 64, axis=1)), axis=0)
+    held = jnp.concatenate((held, side), axis=1)
     for i in range(ZHS):
         moved = pltpu.roll(held, WIDE - HEAD * i, axis=1) if i else held
         for c in range(2):
@@ -391,7 +422,8 @@
             zs.at[2 * to_zh + to_core], zr.at[slot], z_s, z_r, clip=to_zh * YS + y, seq=2 * chip + to_core
         ).start()
     zr[slot] = zs[corner]
-    heads(HEADS // 2, HEADS, *spatial)
+    heads(0, HEADS, *spatial)
+
 
     writes = []
     for n, (low, top) in enumerate(BACK):
@@ -426,7 +458,8 @@
         drain(yfar.at[n], yf_s.at[n])
         for half in range(2):
             drain(yfar.at[n], y_s.at[half, n])
-    drain(xzsend.at[0:(CHIPS - 1) * CHIP_ROWS], xz_s)
+    drain(xzsend.at[0:(CHIPS - 1) * CHIP_ROWS, 0:256], xz_s)
+    drain(rest.at[0:(CHIPS - 1) * REST], xr_s)
     drain(zs.at[0:2 * ZHS - 1], z_s)
     for write in writes:
         write.wait()
@@ -453,7 +486,6 @@
     upstream, space_weight, time_weight,
 ):
     flat = (S, D)
-    time_log = time_logsum.reshape(POS, HEADS, SEQ).transpose(1, 2, 0).reshape(HEADS, S)
     dma = pltpu.SemaphoreType.DMA
     big = jax.ShapeDtypeStruct(flat, BF16)
     small = jax.ShapeDtypeStruct((HEAD, HEAD), F32)
@@ -478,8 +510,9 @@
             pltpu.VMEM((2, HEAD, D), F32),
             pltpu.VMEM((128, D), BF16),
             pltpu.VMEM((S, S), F32),
-            pltpu.VMEM((S, 128), F32),
-            pltpu.VMEM((S, 128), F32),
+            pltpu.VMEM((HEADS, S), F32),
+            pltpu.VMEM((S, 128), BF16),
+            pltpu.VMEM((S, 128), BF16),
             pltpu.VMEM((128, S), F32),
             pltpu.VMEM((128, S), F32),
             pltpu.VMEM((D, S), F32),
@@ -491,13 +524,15 @@
             pltpu.VMEM((2, YROWS // 2, D), BF16),
             pltpu.VMEM((2, YROWS, D), BF16),
             pltpu.VMEM((D, WIDE), BF16),
-            pltpu.VMEM((CHIPS - 1, CHIP_ROWS, WIDE), BF16),
+            pltpu.VMEM((CHIPS - 1, CHIP_ROWS, 256), BF16),
+            pltpu.VMEM((CHIPS * REST, 128), BF16),
+            pltpu.VMEM((CHIPS - 1, REST, 128), BF16),
             pltpu.VMEM((2 * ZHS, ZROWS, 128), BF16),
             pltpu.VMEM((2 * ZHS, ZROWS, 128), BF16),
             dma((9,)), dma((6,)), dma, dma, dma((2,)), dma((2,)), dma, dma,
             dma((2,)), dma((2, 2)), dma((2,)), dma((2,)), dma((2,)), dma((2,)), dma, dma,
             dma((4,)), dma((4,)), dma, dma, dma((3,)), dma((3,)), dma((4,)), dma((4,)),
-            dma((2,)), dma((2,)), dma((2, 2)), dma((2, 2)), dma, dma, dma, dma, dma((3,)),
+            dma((2,)), dma((2,)), dma((2, 2)), dma((2, 2)), dma, dma, dma, dma, dma, dma, dma((3,)),
         ],
         compiler_params=pltpu.CompilerParams(
             collective_id=0, has_side_effects=True, vmem_limit_bytes=60 * 1024 * 1024 - 256 * 1024
@@ -507,7 +542,7 @@
         upstream.reshape(flat), time_query.reshape(flat), time_keys.reshape(flat), time_values.reshape(flat),
         space_output.reshape(flat), time_output.reshape(flat),
         space_query.reshape(flat), space_keys.reshape(flat), space_values.reshape(flat),
-        space_weight, time_weight, space_logsum.reshape(HEADS, S), time_log,
+        space_weight, time_weight, space_logsum.reshape(HEADS, S), time_logsum.reshape(POS, HEADS, SEQ),
     )
     results = pl.pallas_call(
         write_out,

time: 96.8 us -> 90 us (0.930)
  Pallas kernels: 94.3 us -> 89.2 us
  local copies, waits for them, and re-layouts: 1.73 us -> 0 us
    pallas_call x1, Pallas kernels: 91.9 us -> 86.8 us  [shards(): pl.pallas_call(kernel, out_shape=(pltpu.VMEM(flat, BF16),) * 6 + (pltpu.V...]
    transpose x1 -> x0, local copies, waits for them, and re-layouts: 1.02 us -> none  [shards(): time_logsum.reshape(POS, HEADS, SEQ).transpose(1, 2, 0).reshape(HEADS, S)]
where the time goes in v2:
time: 90 us; the launch traced here: 89.9 us
  Pallas kernels  89.2 us (99%)
    pallas_call x1, Pallas kernels, shards(): pl.pallas_call(kernel, out_shape=(pltpu.VMEM(flat, BF16),) * 6 + (pltpu.V...  86.8 us
    pallas_call x1, Pallas kernels, shards(): pl.pallas_call(write_out, out_shape=(big,) * 6 + (small,) * 2, in_specs=[...  2.47 us

profile of v2, /device:TPU:1, one launch (start us, length us, event | category | flops | bytes accessed | tf_op | source)
XLA Modules:
  0.0 89.9 jit_solution(15590642527460877252)
XLA Ops:
  0.6 86.8 %shard_map.188 = (bf16[256,1152]{1,0:T(8,128)(2,1)S(1)}, bf16[256,1152]{1,0:T(8,128)(2,1)S(1)}, bf16[256,1152]{1,0:T(8,128)(2,1)S(1)}, bf16[256,1152]{1,0:T(8,12...) custom-call(bf16[256,1152]{1,0:T(8,128)(2,1)} %bitcast.17, ...), custom_call_target="tpu_custom_call" | custom-call | flops 7000000000 | bytes 12000000 | tf_op jit(solution)/shard_map/pallas_call | solution.py:494
  87.4 2.5 %shard_map.189 = (bf16[256,1152]{1,0:T(8,128)(2,1)}, bf16[256,1152]{1,0:T(8,128)(2,1)}, bf16[256,1152]{1,0:T(8,128)(2,1)}, bf16[256,1152]{1,0:T(8,128)(2,1)}, bf...) custom-call(bf16[256,1152]{1,0:T(8,128)(2,1)S(1)} %get-tuple-element.24.refs_0_, ...), custom_call_target="tpu_custom_call" | custom-call | tf_op jit(solution)/shard_map/pallas_call | solution.py:547

commit v3 on v2

--- a/solution.py
+++ b/solution.py
@@ -22,6 +22,7 @@
 YROWS = ZHS * HEAD
 WIDE = 384
 ZROWS = 80
+PART = 32
 REST = CHIP_ROWS // 3
 GROUPS = ((0, 6), (6, 11), (11, 16))
 FORWARD = ((0, 512), (512, 896), (896, 1152))
@@ -38,10 +39,10 @@
 def kernel(
     up, tq, tk, tv, so, to, sq, sk, sv, ws, wt, slog, tlog,
     osq, osk, osv, otq, otk, otv, ows, owt,
-    X, R, O, SI, GT, GS, TD, TE, W, wown, w32, w32r,
+    X, R, O, SI, GT, GS, TD, TE, W, L, wown, w32, w32r,
     ind, bias, tl, cen, cenr, cent, cens,
     ut, utp, mine, psend, prec, ysend, yfar, yrecv, xzsend, xzrecv, rest, restrecv, zs, zr,
-    ld, own_sem, wp_s, wp_r, w1_s, w1_r, lf_s, lf_r, w2_s, w2_r, wf_s, wf_r, w3_s, w3_r, l3_s, l3_r,
+    ld, own_sem, wp_s, wp_r, w1_s, w1_r, lf_s, lf_r, lg_s, lg_r, l2_s, l2_r, l4_s, l4_r, w2_s, w2_r, wf_s, wf_r, w3_s, w3_r, l3_s, l3_r,
     a_s, a_r, c_s, c_r, b_s, b_r, pp_s, pp_r, yf_s, yf_r, y_s, y_r, xz_s, xz_r, xr_s, xr_r, z_s, z_r, out_sem,
 ):
     clip = lax.axis_index("clip")
@@ -139,10 +140,16 @@
         lax.fori_loop(1, CHIPS, one, 0)
 
     stage1(0)
-    W[core, chip_rows, last] = wown[core, :, last]
+    def part_of(k):
+        return pl.ds(pl.multiple_of(lax.rem(y + k, YS) * PART, PART), PART)
+
+    part, end_rows = part_of(0), pl.ds(YS * PART, CHIP_ROWS - YS * PART)
+    L[chip, part, :] = wown[core, part, last]
+    L[chip, end_rows, :] = wown[core, end_rows, last]
 
     def send_last(k, carry):
-        remote(wown.at[core, :, last], W.at[core, chip_rows, last], lf_s, lf_r, seq=chip_peer(k)).start()
+        remote(wown.at[core, part, last], L.at[chip, part], lf_s, lf_r, seq=chip_peer(k)).start()
+        remote(wown.at[core, end_rows, last], L.at[chip, end_rows], lg_s, lg_r, seq=chip_peer(k)).start()
         return carry
 
     lax.fori_loop(1, CHIPS, send_last, 0)
@@ -260,8 +267,9 @@
     gradient(1)
     far_chunk()
     stage2(0)
-    drain(W.at[0, 0:(CHIPS - 1) * CHIP_ROWS, 0:128], lf_r)
-    remote(W.at[core, :, last], W.at[core, :, last], l3_s, l3_r, seq=sibling).start()
+    drain(L.at[0:CHIPS - 1, 0:PART], lf_r)
+    for n, k in enumerate((1, YS - 1)):
+        remote(L.at[:, part], L.at[:, part], l2_s, l2_r.at[n], clip=y_peer(k)).start()
     for n in (1, 2, 3):
         loads[n].wait()
     forward(0)
@@ -271,8 +279,16 @@
     own_rest.start()
     gradient(3)
     forward2(0)
+    for n, k in enumerate((1, YS - 1)):
+        drain(L.at[:, 0:PART], l2_r.at[n])
+        there = L.at[pl.ds(n * (CHIPS // 2), CHIPS // 2), part_of(YS - k)]
+        remote(there, there, l4_s, l4_r, clip=y_peer(k)).start()
     near_first()
     near_second()
+    drain(L.at[:, 0:PART], l4_r)
+    drain(L.at[0:CHIPS - 1, 0:CHIP_ROWS - YS * PART], lg_r)
+    W[core, :, last] = L[...].reshape(D, 128)
+    remote(W.at[core, :, last], W.at[core, :, last], l3_s, l3_r, seq=sibling).start()
 
     stage3(0)
     drain(W.at[0, :, last], l3_r)
@@ -449,7 +465,10 @@
         drain(W.at[m, :, 0:256], w2_s.at[m])
         drain(W.at[m, :, 0:128], wf_s.at[m])
         drain(W.at[m, :, 0:512], w3_s.at[m])
-    drain(W.at[0, 0:(CHIPS - 1) * CHIP_ROWS, 0:128], lf_s)
+    drain(L.at[0:CHIPS - 1, 0:PART], lf_s)
+    drain(L.at[0:CHIPS - 1, 0:CHIP_ROWS - YS * PART], lg_s)
+    drain(L.at[:, 0:2 * PART], l2_s)
+    drain(L.at[:, 0:PART], l4_s)
     drain(W.at[0, :, 0:128], l3_s)
     drain(cen.at[0:others], c_s)
     for k in range(YS):
@@ -505,6 +524,7 @@
             pltpu.VMEM((3, S, D), BF16),
             pltpu.VMEM((3, S, D), BF16),
             pltpu.VMEM((2, D, D), BF16),
+            pltpu.VMEM((CHIPS, CHIP_ROWS, 128), BF16),
             pltpu.VMEM((2, CHIP_ROWS, D), BF16),
             pltpu.VMEM((2, HEAD, D), F32),
             pltpu.VMEM((2, HEAD, D), F32),
@@ -530,6 +550,7 @@
             pltpu.VMEM((2 * ZHS, ZROWS, 128), BF16),
             pltpu.VMEM((2 * ZHS, ZROWS, 128), BF16),
             dma((9,)), dma((6,)), dma, dma, dma((2,)), dma((2,)), dma, dma,
+            dma, dma, dma, dma((2,)), dma, dma,
             dma((2,)), dma((2, 2)), dma((2,)), dma((2,)), dma((2,)), dma((2,)), dma, dma,
             dma((4,)), dma((4,)), dma, dma, dma((3,)), dma((3,)), dma((4,)), dma((4,)),
             dma((2,)), dma((2,)), dma((2, 2)), dma((2, 2)), dma, dma, dma, dma, dma, dma, dma((3,)),

time: 90 us -> 88.2 us (0.980)
  Pallas kernels: 89.2 us -> 87.5 us
    pallas_call x1, Pallas kernels: 86.8 us -> 85 us  [shards(): pl.pallas_call(kernel, out_shape=(pltpu.VMEM(flat, BF16),) * 6 + (pltpu.V...]
where the time goes in v3:
time: 88.2 us; the launch traced here: 88.1 us
  Pallas kernels  87.5 us (99%)
    pallas_call x1, Pallas kernels, shards(): pl.pallas_call(kernel, out_shape=(pltpu.VMEM(flat, BF16),) * 6 + (pltpu.V...  85 us
    pallas_call x1, Pallas kernels, shards(): pl.pallas_call(write_out, out_shape=(big,) * 6 + (small,) * 2, in_specs=[...  2.47 us

profile of v3, /device:TPU:1, one launch (start us, length us, event | category | flops | bytes accessed | tf_op | source)
XLA Modules:
  0.0 88.1 jit_solution(1350080852888052138)
XLA Ops:
  0.6 85.0 %shard_map.188 = (bf16[256,1152]{1,0:T(8,128)(2,1)S(1)}, bf16[256,1152]{1,0:T(8,128)(2,1)S(1)}, bf16[256,1152]{1,0:T(8,128)(2,1)S(1)}, bf16[256,1152]{1,0:T(8,12...) custom-call(bf16[256,1152]{1,0:T(8,128)(2,1)} %bitcast.17, ...), custom_call_target="tpu_custom_call" | custom-call | flops 7000000000 | bytes 12000000 | tf_op jit(solution)/shard_map/pallas_call | solution.py:513
  85.6 2.5 %shard_map.189 = (bf16[256,1152]{1,0:T(8,128)(2,1)}, bf16[256,1152]{1,0:T(8,128)(2,1)}, bf16[256,1152]{1,0:T(8,128)(2,1)}, bf16[256,1152]{1,0:T(8,128)(2,1)}, bf...) custom-call(bf16[256,1152]{1,0:T(8,128)(2,1)S(1)} %get-tuple-element.24.refs_0_, ...), custom_call_target="tpu_custom_call" | custom-call | tf_op jit(solution)/shard_map/pallas_call | solution.py:568

commit v4 on v3

--- a/solution.py
+++ b/solution.py
@@ -354,7 +354,7 @@
             out[2][:, window] = out[2][:, window] + mm(probs.astype(BF16), g, NN).astype(BF16)
             return carry
 
-        lax.fori_loop(first, end, one, 0)
+        lax.fori_loop(first, end, one, 0, unroll=2 if (end - first) % 2 == 0 else 1)
 
     def over_chips():
         drain(prec.at[0], pp_r.at[0])

time: 88.2 us -> 87.6 us (level)
  no operation moved by 1% of the time
where the time goes in v4:
time: 87.6 us; the launch traced here: 87.5 us
  Pallas kernels  86.8 us (99%)
    pallas_call x1, Pallas kernels, shards(): pl.pallas_call(kernel, out_shape=(pltpu.VMEM(flat, BF16),) * 6 + (pltpu.V...  84.4 us
    pallas_call x1, Pallas kernels, shards(): pl.pallas_call(write_out, out_shape=(big,) * 6 + (small,) * 2, in_specs=[...  2.47 us

profile of v4, /device:TPU:1, one launch (start us, length us, event | category | flops | bytes accessed | tf_op | source)
XLA Modules:
  0.0 87.5 jit_solution(10805131709044492868)
XLA Ops:
  0.6 84.4 %shard_map.188 = (bf16[256,1152]{1,0:T(8,128)(2,1)S(1)}, bf16[256,1152]{1,0:T(8,128)(2,1)S(1)}, bf16[256,1152]{1,0:T(8,128)(2,1)S(1)}, bf16[256,1152]{1,0:T(8,12...) custom-call(bf16[256,1152]{1,0:T(8,128)(2,1)} %bitcast.17, ...), custom_call_target="tpu_custom_call" | custom-call | flops 7000000000 | bytes 12000000 | tf_op jit(solution)/shard_map/pallas_call | solution.py:513
  85.0 2.5 %shard_map.189 = (bf16[256,1152]{1,0:T(8,128)(2,1)}, bf16[256,1152]{1,0:T(8,128)(2,1)}, bf16[256,1152]{1,0:T(8,128)(2,1)}, bf16[256,1152]{1,0:T(8,128)(2,1)}, bf...) custom-call(bf16[256,1152]{1,0:T(8,128)(2,1)S(1)} %get-tuple-element.24.refs_0_, ...), custom_call_target="tpu_custom_call" | custom-call | tf_op jit(solution)/shard_map/pallas_call | solution.py:568
